TPU v7x, 256 devices: a whole 4x4x8 slice. The times are simulated.
256 devices in a mesh: wide: 32 (over x, z_hi, y), narrow: 8 (over z_lo, core).
Axes of the slice: x: 4, y: 4, z: 8 (z_hi: 2, z_lo: 4; z = z_hi * 4 + z_lo), core: 2. Of those that a mesh axis runs over, the one named last changes fastest.
Arguments:
- amplitudes: bfloat16 [65536, 1024], P('wide', 'narrow'), may hold values from -6 to 6
- pair_mask: int32 [512, 8], P('wide', 'narrow'), may hold values 0 or 1
- integrals: bfloat16 [1024, 16384], P('wide', 'narrow'), may hold values from -0.1875 to 0.1875
Outputs:
- ladder: bfloat16 [65536, 16384], P('wide', 'narrow')
All inputs are finite; a program needn't handle non-finite values. No bound on the sum of `pair_mask` on one device may be relied on, other than what follows from the above.
Results may differ from a plain program's by a relative error of at most 0.001.
Values may be sent and summed in bfloat16 or wider, within the bound.
A program may use at most 64 MiB of HBM per device.

v0:
```python
import jax
import jax.numpy as jnp
from jax import lax
from jax.sharding import Mesh
from jax.sharding import PartitionSpec as P

VB = 128
NARROW = ("narrow_0", "narrow_1")
WIDE = ("wide_0", "wide_1", "wide_2")


def sent_to_all(shard, axis):
    length = lax.axis_size(axis)
    return lax.all_to_all(
        jnp.broadcast_to(shard[None], (length, *shard.shape)), axis, 0, 0, tiled=True
    )


def laid_out(tiles, dim):
    tiles = jnp.moveaxis(tiles, 0, dim)
    shape = tiles.shape
    return tiles.reshape(*shape[:dim], shape[dim] * shape[dim + 1], *shape[dim + 2 :])


def gather_axes(shard, axes, dim):
    far, near = axes
    leading = sent_to_all(shard, far)
    tiles = jnp.swapaxes(sent_to_all(leading, near), 0, 1)
    return laid_out(tiles.reshape(-1, *shard.shape), dim)


def gather_in_order(shard, axes, sequence):
    tiles = shard[None]
    for k in sequence:
        tiles = lax.all_gather(tiles, axes[k], axis=0, tiled=True)
    block = [lax.axis_size(axes[k]) for k in reversed(sequence)]
    tiles = tiles.reshape(*block, *shard.shape)
    turned = sorted(range(len(sequence)), key=lambda place: sequence[len(sequence) - 1 - place])
    return tiles.transpose(*turned, *range(len(sequence), tiles.ndim)).reshape(-1, *shard.shape)


def gathered_by_axis(shard, axes, sequence, dim):
    return laid_out(gather_in_order(shard, axes, sequence), dim)


def shards(amplitudes, pair_mask, integrals):
    tiles = jnp.repeat(jnp.repeat(pair_mask, VB, axis=0), VB, axis=1)
    masked = amplitudes * tiles.astype(jnp.bfloat16)
    whole_rows = gather_axes(masked, ("narrow_0", "narrow_1"), 1)
    result = jnp.dot(
        whole_rows,
        gathered_by_axis(integrals, WIDE, (1, 0, 2), 0),
        preferred_element_type=jnp.float32,
    )
    return result.astype(jnp.bfloat16)


def solution(mesh):
    split = Mesh(
        mesh.devices.reshape(4, 2, 4, 4, 2), ("wide_0", "wide_1", "wide_2", "narrow_0", "narrow_1")
    )
    placed = (P(WIDE, NARROW), P(WIDE, NARROW), P(WIDE, NARROW))
    return jax.shard_map(
        shards, mesh=split, in_specs=placed, out_specs=P(WIDE, NARROW), check_vma=False
    )
```

profile of v0, /device:TPU:1, one launch (start us, length us, event | category | flops | bytes accessed | tf_op | source)
XLA Modules:
  0.0 142.3 jit_solution(9726958274767241918)
XLA Ops:
  6.5 0.0 all-gather.4.cloned.1.call-start
  6.5 13.5 %all-gather = bf16[64,2048]{1,0:T(8,128)(2,1)} all-gather(bf16[32,2048]{1,0:T(8,128)(2,1)} %param.5), channel_id=2, replica_groups=mesh['wide_0'=4,'wide_1'=2,'wide_2'=4,'narrow_0'=4,'narrow_1'=2] {'wide_1'}, dimensions={0}, use_global_device_ids=true | all-gather | bytes 393216 | tf_op jit(solution)/shard_map/all_gather | solution.py:35
  20.0 0.0 all-gather.4.cloned.1.call-update
  20.0 0.0 all-gather.6.cloned.1.call-start
  20.1 28.5 %all-gather.4.cloned.1.call-done = bf16[8,32,2048]{2,1,0:T(8,128)(2,1)} async-done(((bf16[2,32,2048]{2,1,0:T(8,128)(2,1)}), bf16[8,32,2048]{2,1,0:T(8,128)(2,1)}) %all-gather.4.cloned.1.call-update) | async-done | bytes 1048592 | tf_op jit(solution)/shard_map/all_gather | solution.py:35
  48.6 0.0 all-gather.6.cloned.1.call-update
  48.6 0.7 convert_bitcast_fusion
  49.3 0.1 broadcast_bitcast_fusion
  49.4 1.4 broadcast_multiply_fusion
  50.7 0.3 broadcast_in_dim.9
  51.0 51.6 %all_to_all.10 = bf16[4,2048,128]{2,1,0:T(8,128)(2,1)S(1)} all-to-all(bf16[4,2048,128]{2,1,0:T(8,128)(2,1)S(1)} %broadcast_in_dim.9), channel_id=1, replica_groups=mesh['wide_0'=4,'wide_1'=2,'wide_2'=4,'narrow_0'=4,'narrow_1'=2] {'narro..., dimensions={0} | all-to-all | bytes 4194304 | tf_op jit(solution)/shard_map/all_to_all | solution.py:14
  102.6 0.5 broadcast_in_dim.10
  103.2 8.6 %all_to_all.11 = bf16[2,4,2048,128]{3,2,1,0:T(8,128)(2,1)S(1)} all-to-all(bf16[2,4,2048,128]{3,2,1,0:T(8,128)(2,1)S(1)} %broadcast_in_dim.10), channel_id=1, replica_groups=mesh['wide_0'=4,'wide_1'=2,'wide_2'=4,'narrow_0'=4,'narrow_1'=2] {'narro..., dimensions={0} | all-to-all | bytes 8388608 | tf_op jit(solution)/shard_map/all_to_all | solution.py:14
  111.8 2.3 %copy.7 = bf16[2,4,2048,128]{3,2,0,1:T(8,128)(2,1)} copy(bf16[2,4,2048,128]{3,2,1,0:T(8,128)(2,1)S(1)} %all_to_all.11) | data formatting | bytes 8388608 | tf_op jit(solution)/shard_map/all_to_all | solution.py:14
  114.1 6.5 %copy.8 = bf16[2048,8,128]{0,2,1:T(8,128)(2,1)} copy(bf16[2048,8,128]{2,0,1:T(8,128)(2,1)} %bitcast.17) | data formatting | bytes 8388608 | tf_op jit(solution)/shard_map/transpose | solution.py:20
  120.6 0.0 all-gather.6.cloned.1.call-done
  120.6 0.0 copy-start
  120.6 2.9 %copy.9 = bf16[4,2,4,32,2048]{4,3,2,1,0:T(8,128)(2,1)S(1)} copy(bf16[4,2,4,32,2048]{4,3,1,0,2:T(8,128)(2,1)} %bitcast.18) | data formatting | bytes 8388608 | tf_op jit(solution)/shard_map/transpose | solution.py:39
  123.5 0.6 copy-done
  124.1 11.4 %convolution_convert_fusion = bf16[2048,2048]{1,0:T(8,128)(2,1)} fusion(bf16[2048,1024]{0,1:T(8,128)(2,1)S(1)} %bitcast.19, bf16[1024,2048]{1,0:T(8,128)(2,1)S(1)} %bitcast.20), kind=kOutput, calls=%fused_computation | convolution fusion | flops 8594128896 | bytes 16777216 | tf_op jit(solution)/shard_map/dot_general | solution.py:50
Async XLA Ops:
  6.5 42.1 %all-gather.4.cloned.1.call-start = ((), (), s32[]{:S(2)}) async-start(), calls=%async_computation.2 | async-start | bytes 1310720 | tf_op jit(solution)/shard_map/all_gather | solution.py:35
  20.0 100.6 %all-gather.6.cloned.1.call-start = ((), (), s32[]{:S(2)}) async-start(), calls=%async_computation.3 | async-start | bytes 5242880 | tf_op jit(solution)/shard_map/all_gather | solution.py:35
  120.6 3.4 %copy-start = (bf16[2048,8,128]{0,2,1:T(8,128)(2,1)S(1)}, bf16[2048,8,128]{0,2,1:T(8,128)(2,1)}, u32[]{:S(2)}) copy-start(bf16[2048,8,128]{0,2,1:T(8,128)(2,1)} %copy.8) | copy-start | bytes 12582916
Sparse Core Ops, SparseCore 0:
  20.2 28.3 all-gather.3
  50.4 52.1 all-gather.5
where the time goes:
time: 143 us; the launch traced here: 142 us
  blocking collectives  73.7 us (52%)
  waiting for transfers between devices  28.5 us (20%)
  between operations  13.4 us (9%)
  local copies, waits for them, and re-layouts  13.2 us (9%)
  matrix products  11.4 us (8%)
  other arithmetic  2.04 us (1%)
    all_to_all x2, blocking collectives, sent_to_all(): lax.all_to_all(jnp.broadcast_to(shard[None], (length, *shard.shape)), axi...  60.2 us
    all_gather x2, waiting for transfers between devices, gather_in_order(): tiles = lax.all_gather(tiles, axes[k], axis=0, tiled=True)  28.5 us
    all_gather x1, blocking collectives, gather_in_order(): tiles = lax.all_gather(tiles, axes[k], axis=0, tiled=True)  13.5 us
    dot_general x1, matrix products, shards(): jnp.dot(whole_rows, gathered_by_axis(integrals, WIDE, (1, 0, 2), 0), pref...  11.4 us
    transpose x1, local copies, waits for them, and re-layouts, laid_out(): tiles = jnp.moveaxis(tiles, 0, dim)  6.52 us
    transpose x1, local copies, waits for them, and re-layouts, gather_in_order(): tiles.transpose(*turned, *range(len(sequence), tiles.ndim))  2.86 us
  transfers between devices with their start and end apart: 2, of which 1 were waited for; matrix products, arithmetic and copies ran while one was open for 8% of the time, Pallas kernels for 0%

commit v1 on v0

--- a/solution.py
+++ b/solution.py
@@ -32,7 +32,9 @@
 def gather_in_order(shard, axes, sequence):
     tiles = shard[None]
     for k in sequence:
-        tiles = lax.all_gather(tiles, axes[k], axis=0, tiled=True)
+        tiles = jnp.concatenate(
+            lax.all_to_all(jnp.stack([tiles] * lax.axis_size(axes[k])), axes[k], 0, 0), axis=0
+        )
     block = [lax.axis_size(axes[k]) for k in reversed(sequence)]
     tiles = tiles.reshape(*block, *shard.shape)
     turned = sorted(range(len(sequence)), key=lambda place: sequence[len(sequence) - 1 - place])

time: 143 us -> 171 us (1.20)
  waiting for transfers between devices: 28.5 us -> 47.8 us
  between operations: 13.4 us -> 0.05 us
  starting transfers between devices: 0.04 us -> 8.85 us
  blocking collectives: 73.7 us -> 82.1 us
  local copies, waits for them, and re-layouts: 13.2 us -> 18.9 us
    all_to_all x0 -> x2, waiting for transfers between devices: none -> 47.8 us  [gather_in_order(): lax.all_to_all(jnp.stack([tiles] * lax.axis_size(axes[k])), axes[k], 0, 0)]
    all_gather x2 -> x0, waiting for transfers between devices: 28.5 us -> none  [gather_in_order(): tiles = lax.all_gather(tiles, axes[k], axis=0, tiled=True)]
    all_to_all x0 -> x1, blocking collectives: none -> 16.8 us  [gather_in_order(): lax.all_to_all(jnp.stack([tiles] * lax.axis_size(axes[k])), axes[k], 0, 0)]
    all_gather x1 -> x0, blocking collectives: 13.5 us -> none  [gather_in_order(): tiles = lax.all_gather(tiles, axes[k], axis=0, tiled=True)]
    all_to_all x0 -> x2, starting transfers between devices: none -> 8.85 us  [gather_in_order(): lax.all_to_all(jnp.stack([tiles] * lax.axis_size(axes[k])), axes[k], 0, 0)]
    all_to_all x2, blocking collectives: 60.2 us -> 65.3 us  [sent_to_all(): lax.all_to_all(jnp.broadcast_to(shard[None], (length, *shard.shape)), axi...]
    another operation x0 -> x2, local copies, waits for them, and re-layouts: none -> 3.59 us  [gather_in_order(): jnp.stack([tiles] * lax.axis_size(axes[k]))]
    transpose x1 -> x0, local copies, waits for them, and re-layouts: 2.86 us -> none  [gather_in_order(): tiles.transpose(*turned, *range(len(sequence), tiles.ndim))]
  transfers between devices with their start and end apart: 2 -> 2, of which waited for: 1 -> 2; matrix products, arithmetic and copies ran while one was open for 8% -> 7% of each run, Pallas kernels for 0% -> 0%
where the time goes in v1:
time: 171 us
  blocking collectives  82.1 us (48%)
  waiting for transfers between devices  47.8 us (28%)
  local copies, waits for them, and re-layouts  18.9 us (11%)
  matrix products  11.4 us (7%)
  starting transfers between devices  8.85 us (5%)
    all_to_all x2, blocking collectives, sent_to_all(): lax.all_to_all(jnp.broadcast_to(shard[None], (length, *shard.shape)), axi...  65.3 us
    all_to_all x2, waiting for transfers between devices, gather_in_order(): lax.all_to_all(jnp.stack([tiles] * lax.axis_size(axes[k])), axes[k], 0, 0)  47.8 us
    all_to_all x1, blocking collectives, gather_in_order(): lax.all_to_all(jnp.stack([tiles] * lax.axis_size(axes[k])), axes[k], 0, 0)  16.8 us
    dot_general x1, matrix products, shards(): jnp.dot(whole_rows, gathered_by_axis(integrals, WIDE, (1, 0, 2), 0), pref...  11.4 us
    all_to_all x2, starting transfers between devices, gather_in_order(): lax.all_to_all(jnp.stack([tiles] * lax.axis_size(axes[k])), axes[k], 0, 0)  8.85 us
    transpose x1, local copies, waits for them, and re-layouts, laid_out(): tiles = jnp.moveaxis(tiles, 0, dim)  6.48 us
    all_to_all x1, local copies, waits for them, and re-layouts, sent_to_all(): lax.all_to_all(jnp.broadcast_to(shard[None], (length, *shard.shape)), axi...  4.5 us
    another operation x2, local copies, waits for them, and re-layouts, gather_in_order(): jnp.stack([tiles] * lax.axis_size(axes[k]))  3.59 us
  transfers between devices with their start and end apart: 2, of which 2 were waited for; matrix products, arithmetic and copies ran while one was open for 7% of the time, Pallas kernels for 0%

profile of v1, /device:TPU:1, one launch (start us, length us, event | category | flops | bytes accessed | tf_op | source)
XLA Modules:
  0.0 170.5 jit_solution(594830260629984350)
XLA Ops:
  0.0 0.0 copy-start.2
  0.0 0.0 copy-start.1
  0.0 1.1 pad_maximum_fusion
  1.1 16.8 %all_to_all.25 = bf16[2,1,32,2048]{3,2,1,0:T(8,128)(2,1)S(1)} all-to-all(bf16[2,1,32,2048]{3,2,1,0:T(8,128)(2,1)S(1)} %pad_maximum_fusion), channel_id=1, replica_groups=mesh['wide_0'=4,'wide_1'=2,'wide_2'=4,'narrow_0'=4,'narrow_1'=2] {'wide_1'}, dimensions={0} | all-to-all | bytes 524288 | tf_op jit(solution)/shard_map/all_to_all | solution.py:36
  17.9 1.1 stack.10
  19.0 4.0 %all-to-all-start.3 = ((bf16[4,2,32,2048]{3,2,1,0:T(8,128)(2,1)}), bf16[4,2,32,2048]{3,2,1,0:T(8,128)(2,1)S(1)}, u32[]{:S(2)}, u32[]{:S(2)}) async-start(bf16[4,2,32,2048]{3,2,1,0:T(8,128)(2,1)} %stack.10), calls=%async_computation.3 | async-start | bytes 2097152 | tf_op jit(solution)/shard_map/all_to_all | solution.py:36
  23.0 0.0 copy-done.2
  23.0 0.1 broadcast_bitcast_fusion
  23.1 0.0 copy-done.1
  23.1 0.3 broadcast_multiply_fusion
  23.4 10.2 %all-to-all-done.3 = bf16[4,2,32,2048]{3,2,1,0:T(8,128)(2,1)S(1)} async-done(((bf16[4,2,32,2048]{3,2,1,0:T(8,128)(2,1)}), bf16[4,2,32,2048]{3,2,1,0:T(8,128)(2,1)S(1)}, u32[]{:S(2)}, u32[]{:S(2)}) %all-to-all-start.3) | async-done | bytes 1048608 | tf_op jit(solution)/shard_map/all_to_all | solution.py:36
  33.6 0.3 broadcast_in_dim.7
  33.9 55.3 %all_to_all.26 = bf16[4,2048,128]{2,1,0:T(8,128)(2,1)S(1)} all-to-all(bf16[4,2048,128]{2,1,0:T(8,128)(2,1)S(1)} %broadcast_in_dim.7), channel_id=1, replica_groups=mesh['wide_0'=4,'wide_1'=2,'wide_2'=4,'narrow_0'=4,'narrow_1'=2] {'narro..., dimensions={0} | all-to-all | bytes 4194304 | tf_op jit(solution)/shard_map/all_to_all | solution.py:14
  89.3 0.5 broadcast_in_dim.8
  89.8 9.9 %all_to_all.27 = bf16[2,4,2048,128]{3,2,1,0:T(8,128)(2,1)} all-to-all(bf16[2,4,2048,128]{3,2,1,0:T(8,128)(2,1)S(1)} %broadcast_in_dim.8), channel_id=1, replica_groups=mesh['wide_0'=4,'wide_1'=2,'wide_2'=4,'narrow_0'=4,'narrow_1'=2] {'narro..., dimensions={0} | all-to-all | bytes 8388608 | tf_op jit(solution)/shard_map/all_to_all | solution.py:14
  99.7 2.5 %stack.11 = bf16[4,8,32,2048]{3,2,1,0:T(8,128)(2,1)} broadcast(bf16[8,32,2048]{2,1,0:T(8,128)(2,1)S(1)} %bitcast.21), dimensions={1,2,3} | broadcast | bytes 5242880 | tf_op jit(solution)/shard_map/stack | solution.py:36
  102.2 4.8 %all-to-all-start.4 = ((bf16[4,8,32,2048]{3,2,1,0:T(8,128)(2,1)}), bf16[4,8,32,2048]{3,2,1,0:T(8,128)(2,1)}, u32[]{:S(2)}, u32[]{:S(2)}) async-start(bf16[4,8,32,2048]{3,2,1,0:T(8,128)(2,1)} %stack.11), calls=%async_computation.4 | async-start | bytes 8388608 | tf_op jit(solution)/shard_map/all_to_all | solution.py:36
  107.1 4.5 %copy.5 = bf16[2,4,2048,128]{3,2,0,1:T(8,128)(2,1)} copy(bf16[2,4,2048,128]{3,2,1,0:T(8,128)(2,1)} %all_to_all.27) | data formatting | bytes 8388608 | tf_op jit(solution)/shard_map/all_to_all | solution.py:14
  111.6 6.5 %copy.6 = bf16[2048,8,128]{0,2,1:T(8,128)(2,1)} copy(bf16[2048,8,128]{2,0,1:T(8,128)(2,1)} %bitcast.20) | data formatting | bytes 8388608 | tf_op jit(solution)/shard_map/transpose | solution.py:20
  118.0 37.6 %all-to-all-done.4 = bf16[4,8,32,2048]{3,2,1,0:T(8,128)(2,1)} async-done(((bf16[4,8,32,2048]{3,2,1,0:T(8,128)(2,1)}), bf16[4,8,32,2048]{3,2,1,0:T(8,128)(2,1)}, u32[]{:S(2)}, u32[]{:S(2)}) %all-to-all-start.4) | async-done | bytes 4194336 | tf_op jit(solution)/shard_map/all_to_all | solution.py:36
  155.7 0.0 copy-start
  155.7 2.9 %copy.7 = bf16[4,8,32,2048]{3,2,0,1:T(8,128)(2,1)S(1)} copy(bf16[4,8,32,2048]{3,2,1,0:T(8,128)(2,1)} %all-to-all-done.4) | data formatting | bytes 8388608 | tf_op jit(solution)/shard_map/all_to_all | solution.py:36
  158.5 0.6 copy-done
  159.1 11.4 %convolution_convert_fusion = bf16[2048,2048]{1,0:T(8,128)(2,1)} fusion(bf16[2048,1024]{0,1:T(8,128)(2,1)S(1)} %bitcast.22, bf16[1024,2048]{1,0:T(8,128)(2,1)S(1)} %bitcast.23), kind=kOutput, calls=%fused_computation | convolution fusion | flops 8594128896 | bytes 16777216 | tf_op jit(solution)/shard_map/dot_general | solution.py:52
  (1 shorter events, 0.0 us)
Async XLA Ops:
  0.0 23.0 %copy-start.2 = (s32[16,1]{0,1:T(1,128)S(1)}, s32[16,1]{0,1:T(1,128)}, u32[]{:S(2)}) copy-start(s32[16,1]{0,1:T(1,128)} %param.4) | copy-start | bytes 196
  0.0 23.1 %copy-start.1 = (bf16[2048,128]{1,0:T(8,128)(2,1)S(1)}, bf16[2048,128]{1,0:T(8,128)(2,1)}, u32[]{:S(2)}) copy-start(bf16[2048,128]{1,0:T(8,128)(2,1)} %param.3) | copy-start | bytes 1572868
  19.0 14.7 %all-to-all-start.3 = ((bf16[4,2,32,2048]{3,2,1,0:T(8,128)(2,1)}), bf16[4,2,32,2048]{3,2,1,0:T(8,128)(2,1)S(1)}, u32[]{:S(2)}, u32[]{:S(2)}) async-start(bf16[4,2,32,2048]{3,2,1,0:T(8,128)(2,1)} %stack.10), calls=%async_computation.3 | async-start | bytes 2097152 | tf_op jit(solution)/shard_map/all_to_all | solution.py:36
  102.2 53.5 %all-to-all-start.4 = ((bf16[4,8,32,2048]{3,2,1,0:T(8,128)(2,1)}), bf16[4,8,32,2048]{3,2,1,0:T(8,128)(2,1)}, u32[]{:S(2)}, u32[]{:S(2)}) async-start(bf16[4,8,32,2048]{3,2,1,0:T(8,128)(2,1)} %stack.11), calls=%async_computation.4 | async-start | bytes 8388608 | tf_op jit(solution)/shard_map/all_to_all | solution.py:36
  155.7 3.4 %copy-start = (bf16[2048,8,128]{0,2,1:T(8,128)(2,1)S(1)}, bf16[2048,8,128]{0,2,1:T(8,128)(2,1)}, u32[]{:S(2)}) copy-start(bf16[2048,8,128]{0,2,1:T(8,128)(2,1)} %copy.6) | copy-start | bytes 12582916
